TPU v7x, 512 devices: a whole 4x4x16 slice. The times are simulated.
512 devices in a mesh: ctx: 64 (over x, z), tp: 8 (over y, core).
Axes of the slice: x: 4, y: 4, z: 16, core: 2. Of those that a mesh axis runs over, the one named last changes fastest.
Arguments:
- query_in: bfloat16 [12288, 8192], P(('ctx', 'tp')), may hold values from -150 to 150
- key_in: bfloat16 [12288, 1024], P(('ctx', 'tp')), may hold values from -8 to 8
- value_in: bfloat16 [12288, 1024], P(('ctx', 'tp')), may hold values from -6 to 6
- grad_out: bfloat16 [12288, 8192], P(('ctx', 'tp')), may hold values from -24 to 24
- segments: int32 [12288], P('ctx'), may hold values from 0 to 61, as said below
Outputs:
- attn_out: bfloat16 [12288, 8192], P(('ctx', 'tp'))
- grad_query: bfloat16 [12288, 8192], P(('ctx', 'tp'))
- grad_key: bfloat16 [12288, 1024], P(('ctx', 'tp'))
- grad_value: bfloat16 [12288, 1024], P(('ctx', 'tp'))
Inputs may be any that keep to these rules, and one draw needn't show every extreme that they name: `segments`: ids start at 0 and never fall along the tokens; each document holds at most 768 tokens, and one holds exactly that many.
All inputs are finite; a program needn't handle non-finite values.
Results may differ from a plain program's by a relative error of at most 0.03.
Values may be sent and summed in bfloat16 or wider, within the bound.
A program may use at most 64 MiB of HBM per device.

v0:
```python
import math

import jax
import jax.numpy as jnp
from jax import lax
from jax.sharding import PartitionSpec as P

HEADS = 64
KV_HEADS = 8
HEAD_DIM = 128
SPAN = 4


def prefix(array, axis, combine, identity):
    length, place = (lax.axis_size(axis), lax.axis_index(axis))
    everything = jax.tree.map(lambda part: lax.all_gather(part, axis), array)
    start = jax.tree.map(
        lambda part, zero: jnp.broadcast_to(jnp.asarray(zero, part.dtype), part.shape),
        array,
        identity,
    )

    def step(k, before):
        reached = k < place
        new = combine(before, jax.tree.map(lambda part: part[k], everything))
        return jax.tree.map(lambda a, b: jnp.where(reached, a, b), new, before)

    return lax.fori_loop(0, length, step, start)


def shifted(block, axis, distance):
    devices = range(lax.axis_size(axis))
    route = [(i - distance, i) for i in devices if i - distance in devices]
    return lax.ppermute(block, axis, route)


def join_docs(earlier, later):
    early_seg, early_start = earlier
    late_seg, late_start = later
    absent = late_seg < 0
    joined = early_seg == late_seg
    seg_out = jnp.where(absent, early_seg, late_seg)
    start_out = jnp.where(absent | joined, early_start, late_start)
    return (seg_out, start_out)


def block_scores(query_four, key_block, doc_first, query_pos, key_pos, scaling):
    scores = (
        jnp.einsum("tkgd,skd->kgts", query_four, key_block, preferred_element_type=jnp.float32)
        * scaling
    )
    visible = (key_pos[None, :] >= doc_first[:, None]) & (key_pos[None, :] <= query_pos[:, None])
    return jnp.where(visible[None, None], scores, -jnp.inf)


def block_terms(
    query_four,
    grad_four,
    log_total,
    row_dot,
    doc_first,
    query_pos,
    key_block,
    value_block,
    key_pos,
    scaling,
):
    scores = block_scores(query_four, key_block, doc_first, query_pos, key_pos, scaling)
    probs = jnp.exp(scores - log_total[..., None])
    probs_low = probs.astype(jnp.bfloat16)
    dprobs = jnp.einsum(
        "tkgd,skd->kgts", grad_four, value_block, preferred_element_type=jnp.float32
    )
    dscores = (probs * (dprobs - row_dot[..., None])).astype(jnp.bfloat16)
    return (probs_low, dscores)


def key_terms(probs_low, dscores, queries, grads, scaling):
    key_term = (
        jnp.einsum("kgts,tkgd->skd", dscores, queries, preferred_element_type=jnp.float32) * scaling
    )
    value_term = jnp.einsum("kgts,tkgd->skd", probs_low, grads, preferred_element_type=jnp.float32)
    return (key_term, value_term)


def body(query_in, key_in, value_in, grad_out, segments):
    query_heads, key_heads, value_heads, grad_heads = (
        lax.all_to_all(query_in, "tp", split_axis=1, concat_axis=0, tiled=True),
        lax.all_to_all(key_in, "tp", split_axis=1, concat_axis=0, tiled=True),
        lax.all_to_all(value_in, "tp", split_axis=1, concat_axis=0, tiled=True),
        lax.all_to_all(grad_out, "tp", split_axis=1, concat_axis=0, tiled=True),
    )
    tok_rows = query_heads.shape[0]
    head_width = HEAD_DIM
    kv_local = key_heads.shape[1] // head_width
    groups = HEADS // KV_HEADS
    scaling = 1.0 / math.sqrt(head_width)
    stretch_index = lax.axis_index("ctx")
    ctx_size = lax.axis_size("ctx")
    offsets = jnp.arange(tok_rows, dtype=jnp.int32)
    query_pos = stretch_index * tok_rows + offsets
    same_doc = segments[:, None] == segments[None, :]
    local_first = jnp.min(jnp.where(same_doc, query_pos[None, :], jnp.int32(1 << 30)), axis=1)
    prev_seg, prev_start = prefix(
        (segments[-1:], local_first[-1:]),
        "ctx",
        join_docs,
        (jnp.full((1,), -1, jnp.int32), jnp.zeros((1,), jnp.int32)),
    )
    doc_first = jnp.where(segments == prev_seg, prev_start, local_first)
    query_four = query_heads.reshape(tok_rows, kv_local, groups, head_width)
    grad_four = grad_heads.reshape(tok_rows, kv_local, groups, head_width)
    key_list = [key_heads]
    value_list = [value_heads]
    for distance in range(1, SPAN + 1):
        got_keys, got_values = shifted((key_heads, value_heads), "ctx", distance)
        key_list.append(got_keys)
        value_list.append(got_values)
    key_stack = jnp.stack(key_list)
    value_stack = jnp.stack(value_list)
    key_stack = key_stack.reshape(SPAN + 1, tok_rows, kv_local, head_width)
    value_stack = value_stack.reshape(SPAN + 1, tok_rows, kv_local, head_width)
    first_least = jnp.min(doc_first)

    def key_pos_at(block_index):
        return (stretch_index - block_index) * tok_rows + offsets

    def needed_at(block_index):
        return first_least < (stretch_index - block_index + 1) * tok_rows

    def scores_at(block_index):
        return block_scores(
            query_four,
            key_stack[block_index],
            doc_first,
            query_pos,
            key_pos_at(block_index),
            scaling,
        )

    base_scores = scores_at(0)
    row_max = jnp.max(base_scores, axis=-1)
    row_total = jnp.sum(jnp.exp(base_scores - row_max[..., None]), axis=-1)
    for distance in range(1, SPAN + 1):

        def update_total(carried, distance=distance):
            old_max, old_total = carried
            scores = scores_at(distance)
            new_max = jnp.maximum(old_max, jnp.max(scores, axis=-1))
            fresh = jnp.sum(jnp.exp(scores - new_max[..., None]), axis=-1)
            return (new_max, old_total * jnp.exp(old_max - new_max) + fresh)

        row_max, row_total = lax.cond(
            needed_at(distance), update_total, lambda carried: carried, (row_max, row_total)
        )
    log_total = row_max + jnp.log(row_total)
    running = jnp.zeros((tok_rows, kv_local, groups, head_width), jnp.float32)
    for distance in range(SPAN + 1):

        def add_output(carried, distance=distance):
            probs_low = jnp.exp(scores_at(distance) - log_total[..., None]).astype(jnp.bfloat16)
            return carried + jnp.einsum(
                "kgts,skd->tkgd",
                probs_low,
                value_stack[distance],
                preferred_element_type=jnp.float32,
            )

        if distance == 0:
            running = add_output(running)
        else:
            running = lax.cond(needed_at(distance), add_output, lambda carried: carried, running)
    out_heads = running.astype(jnp.bfloat16)
    row_dot = jnp.sum(
        grad_four.astype(jnp.float32) * out_heads.astype(jnp.float32), axis=-1
    ).transpose(1, 2, 0)

    def local_terms(block_index):
        return block_terms(
            query_four,
            grad_four,
            log_total,
            row_dot,
            doc_first,
            query_pos,
            key_stack[block_index],
            value_stack[block_index],
            key_pos_at(block_index),
            scaling,
        )

    def query_term(dscores, block_index):
        return jnp.einsum(
            "kgts,skd->tkgd", dscores, key_stack[block_index], preferred_element_type=jnp.float32
        )

    probs_low, dscores = local_terms(0)
    grad_q = query_term(dscores, 0)
    grad_k, grad_v = key_terms(probs_low, dscores, query_four, grad_four, scaling)
    for distance in range(1, SPAN + 1):

        def near_query(carried, distance=distance):
            near_probs, near_dscores = local_terms(distance)
            return carried + query_term(near_dscores, distance)

        grad_q = lax.cond(needed_at(distance), near_query, lambda carried: carried, grad_q)
    first_float = doc_first.astype(jnp.float32)
    own_keys = key_stack[0]
    own_values = value_stack[0]
    own_pos = key_pos_at(0)
    last_key = (stretch_index * tok_rows + tok_rows - 1).astype(jnp.float32)
    for distance in range(1, SPAN + 1):
        got_queries, got_grads = shifted((query_heads, grad_heads), "ctx", -distance)
        got_total, got_dot, got_first = shifted((log_total, row_dot, first_float), "ctx", -distance)

        def key_side(
            carried,
            distance=distance,
            got_queries=got_queries,
            got_grads=got_grads,
            got_total=got_total,
            got_dot=got_dot,
            got_first=got_first,
        ):
            their_four = got_queries.reshape(tok_rows, kv_local, groups, head_width)
            their_grads = got_grads.reshape(tok_rows, kv_local, groups, head_width)
            their_pos = (stretch_index + distance) * tok_rows + offsets
            their_probs, their_dscores = block_terms(
                their_four,
                their_grads,
                got_total,
                got_dot,
                got_first.astype(jnp.int32),
                their_pos,
                own_keys,
                own_values,
                own_pos,
                scaling,
            )
            key_term, value_term = key_terms(
                their_probs, their_dscores, their_four, their_grads, scaling
            )
            return (carried[0] + key_term, carried[1] + value_term)

        inside = (stretch_index + distance < ctx_size) & (jnp.min(got_first) <= last_key)
        grad_k, grad_v = lax.cond(inside, key_side, lambda carried: carried, (grad_k, grad_v))
    out_flat = out_heads.reshape(tok_rows, kv_local * groups * head_width)
    query_flat = (
        (grad_q * scaling).astype(jnp.bfloat16).reshape(tok_rows, kv_local * groups * head_width)
    )
    key_flat = grad_k.astype(jnp.bfloat16).reshape(tok_rows, kv_local * head_width)
    value_flat = grad_v.astype(jnp.bfloat16).reshape(tok_rows, kv_local * head_width)
    attn_out, grad_query, grad_key, grad_value = (
        lax.all_to_all(out_flat, "tp", split_axis=0, concat_axis=1, tiled=True),
        lax.all_to_all(query_flat, "tp", split_axis=0, concat_axis=1, tiled=True),
        lax.all_to_all(key_flat, "tp", split_axis=0, concat_axis=1, tiled=True),
        lax.all_to_all(value_flat, "tp", split_axis=0, concat_axis=1, tiled=True),
    )
    return (attn_out, grad_query, grad_key, grad_value)


def solution(mesh):
    placed = (
        P(("ctx", "tp"), None),
        P(("ctx", "tp"), None),
        P(("ctx", "tp"), None),
        P(("ctx", "tp"), None),
        P("ctx"),
    )
    return jax.shard_map(
        body,
        mesh=mesh,
        in_specs=placed,
        out_specs=(
            P(("ctx", "tp"), None),
            P(("ctx", "tp"), None),
            P(("ctx", "tp"), None),
            P(("ctx", "tp"), None),
        ),
        check_vma=False,
    )
```

profile of v0, /device:TPU:1, one launch (start us, length us, event | category | flops | bytes accessed | tf_op | source)
XLA Modules:
  0.0 570.7 jit_solution(8409792215185441054)
XLA Ops:
  2.1 10.1 %all-to-all-start = ((bf16[24,8,128]{2,0,1:T(8,128)(2,1)}), bf16[24,8,128]{2,0,1:T(8,128)(2,1)S(1)}, u32[]{:S(2)}, u32[]{:S(2)}) async-start(bf16[24,8,128]{2,0,1:T(8,128)(2,1)} %copy_bitcast_fusion.5), calls=%async_computation | async-start | bytes 98304 | tf_op jit(solution)/shard_map/all_to_all | solution.py:89
  16.8 24.8 %all-reduce.2 = (s32[64]{0:T(128)S(1)}, s32[64]{0:T(128)S(1)}) all-reduce(s32[64]{0:T(128)S(1)} %slice_dynamic-update-slice_fusion.1, s32[64]{0:T(128)S(1)} %slice_dynamic-update-slice_fusion), channel_id=2, replica_groups=mesh['ctx'=64,'tp'=8] {'ctx'}, use_global_device_ids=true, to_apply=%add | all-reduce | flops 128 | bytes 1024
  41.6 207.9 %while.15 = (s32[]{:T(128)}, s32[1]{0:T(128)}, s32[1]{0:T(128)}, s32[]{:T(128)}, s32[64,1]{0,1:T(1,128)S(1)}, /*index=5*/s32[64,1]{0,1:T(1,128)S(1)}, s32[]{:T(128)}, s32[1]{0:T(128)}) while((s32[]{:T(128)}, s32[1]{0:T(128)}, s32[1]{0:T(128)}, s32[]{:T(128)}, s32[64,1]{0,1:T(1,128)S(1)}, /*index=5*/s32[64,1]{0,1:T(1,128)S(1)}, s32[]{:T(128)}, ...), condition=%wide.region_2.3_spmd, body=%wide.region_1.2_spmd.sunk | while | flops 10 | bytes 187 | solution.py:28
  251.7 1.8 copy.577
  257.5 10.0 %all-to-all-start.2 = ((bf16[24,8,128]{2,0,1:T(8,128)(2,1)}), bf16[24,8,128]{2,0,1:T(8,128)(2,1)S(1)}, u32[]{:S(2)}, u32[]{:S(2)}) async-start(bf16[24,8,128]{2,0,1:T(8,128)(2,1)} %copy_bitcast_fusion.4), calls=%async_computation.2 | async-start | bytes 98304 | tf_op jit(solution)/shard_map/all_to_all | solution.py:90
  267.5 2.6 collective-permute-start
  270.2 3.1 collective-permute-start.1
  273.2 4.7 collective-permute-start.2
  278.0 2.4 collective-permute-start.3
  280.4 5.7 all-to-all-start.1
  286.1 2.1 collective-permute-start.4
  288.2 1.9 collective-permute-start.5
  290.2 8.0 %collective-permute-start.6 = (bf16[192,128]{1,0:T(8,128)(2,1)S(1)}, bf16[192,128]{1,0:T(8,128)(2,1)S(1)}, u32[]{:S(2)}, u32[]{:S(2)}) collective-permute-start(bf16[192,128]{1,0:T(8,128)(2,1)S(1)} %bitcast.1085), channel_id=1, source_target_pairs={{0,24},{8,32},{16,40},{24,48},{32,56},{40,64},{48,72},{56,80},{64,... | collective-permute-start | bytes 147464 | tf_op jit(solution)/shard_map/ppermute | solution.py:34
  298.2 5.2 collective-permute-start.7
  304.6 7.1 %all-to-all-start.4 = ((bf16[24,8,1024]{2,0,1:T(8,128)(2,1)}), bf16[24,8,1024]{2,0,1:T(8,128)(2,1)}, u32[]{:S(2)}, u32[]{:S(2)}) async-start(bf16[24,8,1024]{2,0,1:T(8,128)(2,1)} %bitcast.1044), calls=%async_computation.4 | async-start | bytes 786432 | tf_op jit(solution)/shard_map/all_to_all | solution.py:91
  316.7 3.1 all-to-all-done.4
  326.3 4.8 all-to-all-start.5
  333.8 9.1 %collective-permute-done.11 = f32[192]{0:T(256)S(1)} collective-permute-done((f32[192]{0:T(256)S(1)}, f32[192]{0:T(256)S(1)}, u32[]{:S(2)}, u32[]{:S(2)}) %collective-permute-start.11) | collective-permute-done | bytes 800 | tf_op jit(solution)/shard_map/ppermute | solution.py:34
  344.1 6.0 %collective-permute-done.10 = f32[192]{0:T(256)S(1)} collective-permute-done((f32[192]{0:T(256)S(1)}, f32[192]{0:T(256)S(1)}, u32[]{:S(2)}, u32[]{:S(2)}) %collective-permute-start.10) | collective-permute-done | bytes 800 | tf_op jit(solution)/shard_map/ppermute | solution.py:34
  351.4 6.8 %collective-permute-done.9 = f32[192]{0:T(256)S(1)} collective-permute-done((f32[192]{0:T(256)S(1)}, f32[192]{0:T(256)S(1)}, u32[]{:S(2)}, u32[]{:S(2)}) %collective-permute-start.9) | collective-permute-done | bytes 800 | tf_op jit(solution)/shard_map/ppermute | solution.py:34
  359.5 17.9 %collective-permute-done.8 = f32[192]{0:T(256)S(1)} collective-permute-done((f32[192]{0:T(256)S(1)}, f32[192]{0:T(256)S(1)}, u32[]{:S(2)}, u32[]{:S(2)}) %collective-permute-start.8) | collective-permute-done | bytes 800 | tf_op jit(solution)/shard_map/ppermute | solution.py:34
  380.0 1.8 collective-permute-done.13
  383.1 4.2 collective-permute-done.19
  390.4 6.6 %collective-permute-done.23 = f32[1,8,192]{1,2,0:T(8,128)S(1)} collective-permute-done((f32[1,8,192]{1,2,0:T(8,128)S(1)}, f32[1,8,192]{1,2,0:T(8,128)S(1)}, u32[]{:S(2)}, u32[]{:S(2)}) %collective-permute-start.23) | collective-permute-done | bytes 6176 | tf_op jit(solution)/shard_map/ppermute | solution.py:34
  410.6 9.2 %all-to-all-start.3 = ((bf16[8,24,1024]{2,1,0:T(8,128)(2,1)}), bf16[8,24,1024]{2,1,0:T(8,128)(2,1)}, u32[]{:S(2)}, u32[]{:S(2)}) async-start(bf16[8,24,1024]{2,1,0:T(8,128)(2,1)} %all_to_all.117), calls=%async_computation.3 | async-start | bytes 786432 | tf_op jit(solution)/shard_map/all_to_all | solution.py:254
  421.5 18.3 %collective-permute-done.20 = bf16[192,1024]{1,0:T(8,128)(2,1)} collective-permute-done((bf16[192,1024]{1,0:T(8,128)(2,1)}, bf16[192,1024]{1,0:T(8,128)(2,1)}, u32[]{:S(2)}, u32[]{:S(2)}) %collective-permute-start.20) | collective-permute-done | bytes 393248 | tf_op jit(solution)/shard_map/ppermute | solution.py:34
  441.5 4.9 conditional.28
  446.4 34.5 %collective-permute-done.22 = bf16[192,1024]{1,0:T(8,128)(2,1)} collective-permute-done((bf16[192,1024]{1,0:T(8,128)(2,1)}, bf16[192,1024]{1,0:T(8,128)(2,1)}, u32[]{:S(2)}, u32[]{:S(2)}) %collective-permute-start.22) | collective-permute-done | bytes 393248 | tf_op jit(solution)/shard_map/ppermute | solution.py:34
  480.9 66.7 %collective-permute-done.27 = f32[1,8,192]{1,2,0:T(8,128)S(1)} collective-permute-done((f32[1,8,192]{1,2,0:T(8,128)S(1)}, f32[1,8,192]{1,2,0:T(8,128)S(1)}, u32[]{:S(2)}, u32[]{:S(2)}) %collective-permute-start.27) | collective-permute-done | bytes 6176 | tf_op jit(solution)/shard_map/ppermute | solution.py:34
  548.4 7.9 %all-to-all-start.7 = ((bf16[8,24,128]{2,1,0:T(8,128)(2,1)}), bf16[8,24,128]{2,1,0:T(8,128)(2,1)S(1)}, u32[]{:S(2)}, u32[]{:S(2)}) async-start(bf16[8,24,128]{2,1,0:T(8,128)(2,1)} %bitcast.324), calls=%async_computation.7 | async-start | bytes 98304 | tf_op jit(solution)/shard_map/all_to_all | solution.py:257
  561.1 4.2 all-to-all-start.6
  565.9 4.2 all-to-all-done.6
  (217 shorter events, 103.1 us)
Async XLA Ops:
  2.1 255.4 %all-to-all-start = ((bf16[24,8,128]{2,0,1:T(8,128)(2,1)}), bf16[24,8,128]{2,0,1:T(8,128)(2,1)S(1)}, u32[]{:S(2)}, u32[]{:S(2)}) async-start(bf16[24,8,128]{2,0,1:T(8,128)(2,1)} %copy_bitcast_fusion.5), calls=%async_computation | async-start | bytes 98304 | tf_op jit(solution)/shard_map/all_to_all | solution.py:89
  257.5 22.9 %all-to-all-start.2 = ((bf16[24,8,128]{2,0,1:T(8,128)(2,1)}), bf16[24,8,128]{2,0,1:T(8,128)(2,1)S(1)}, u32[]{:S(2)}, u32[]{:S(2)}) async-start(bf16[24,8,128]{2,0,1:T(8,128)(2,1)} %copy_bitcast_fusion.4), calls=%async_computation.2 | async-start | bytes 98304 | tf_op jit(solution)/shard_map/all_to_all | solution.py:90
  267.5 20.7 %collective-permute-start = (bf16[192,128]{1,0:T(8,128)(2,1)S(1)}, bf16[192,128]{1,0:T(8,128)(2,1)S(1)}, u32[]{:S(2)}, u32[]{:S(2)}) collective-permute-start(bf16[192,128]{1,0:T(8,128)(2,1)S(1)} %bitcast.1123), channel_id=1, source_target_pairs={{0,8},{8,16},{16,24},{24,32},{32,40},{40,48},{48,56},{56,64},{64,7... | collective-permute-start | bytes 147464 | tf_op jit(solution)/shard_map/ppermute | solution.py:34
  270.2 20.0 %collective-permute-start.1 = (bf16[192,128]{1,0:T(8,128)(2,1)S(1)}, bf16[192,128]{1,0:T(8,128)(2,1)S(1)}, u32[]{:S(2)}, u32[]{:S(2)}) collective-permute-start(bf16[192,128]{1,0:T(8,128)(2,1)S(1)} %bitcast.1124), channel_id=1, source_target_pairs={{0,16},{8,24},{16,32},{24,40},{32,48},{40,56},{48,64},{56,72},{64,... | collective-permute-start | bytes 147464 | tf_op jit(solution)/shard_map/ppermute | solution.py:34
  273.2 24.9 %collective-permute-start.2 = (bf16[192,128]{1,0:T(8,128)(2,1)S(1)}, bf16[192,128]{1,0:T(8,128)(2,1)S(1)}, u32[]{:S(2)}, u32[]{:S(2)}) collective-permute-start(bf16[192,128]{1,0:T(8,128)(2,1)S(1)} %bitcast.1125), channel_id=1, source_target_pairs={{0,24},{8,32},{16,40},{24,48},{32,56},{40,64},{48,72},{56,80},{64,... | collective-permute-start | bytes 147464 | tf_op jit(solution)/shard_map/ppermute | solution.py:34
  278.0 25.4 %collective-permute-start.3 = (bf16[192,128]{1,0:T(8,128)(2,1)S(1)}, bf16[192,128]{1,0:T(8,128)(2,1)S(1)}, u32[]{:S(2)}, u32[]{:S(2)}) collective-permute-start(bf16[192,128]{1,0:T(8,128)(2,1)S(1)} %bitcast.1126), channel_id=1, source_target_pairs={{0,32},{8,40},{16,48},{24,56},{32,64},{40,72},{48,80},{56,88},{64,... | collective-permute-start | bytes 147464 | tf_op jit(solution)/shard_map/ppermute | solution.py:34
  280.4 24.1 %all-to-all-start.1 = ((bf16[24,8,1024]{2,0,1:T(8,128)(2,1)}), bf16[24,8,1024]{2,0,1:T(8,128)(2,1)}, u32[]{:S(2)}, u32[]{:S(2)}) async-start(bf16[24,8,1024]{2,0,1:T(8,128)(2,1)} %bitcast.1045), calls=%async_computation.1 | async-start | bytes 786432 | tf_op jit(solution)/shard_map/all_to_all | solution.py:88
  286.1 17.4 %collective-permute-start.4 = (bf16[192,128]{1,0:T(8,128)(2,1)S(1)}, bf16[192,128]{1,0:T(8,128)(2,1)S(1)}, u32[]{:S(2)}, u32[]{:S(2)}) collective-permute-start(bf16[192,128]{1,0:T(8,128)(2,1)S(1)} %bitcast.1082), channel_id=1, source_target_pairs={{0,8},{8,16},{16,24},{24,32},{32,40},{40,48},{48,56},{56,64},{64,7... | collective-permute-start | bytes 147464 | tf_op jit(solution)/shard_map/ppermute | solution.py:34
  288.2 15.2 %collective-permute-start.5 = (bf16[192,128]{1,0:T(8,128)(2,1)S(1)}, bf16[192,128]{1,0:T(8,128)(2,1)S(1)}, u32[]{:S(2)}, u32[]{:S(2)}) collective-permute-start(bf16[192,128]{1,0:T(8,128)(2,1)S(1)} %bitcast.1084), channel_id=1, source_target_pairs={{0,16},{8,24},{16,32},{24,40},{32,48},{40,56},{48,64},{56,72},{64,... | collective-permute-start | bytes 147464 | tf_op jit(solution)/shard_map/ppermute | solution.py:34
  290.2 13.3 %collective-permute-start.6 = (bf16[192,128]{1,0:T(8,128)(2,1)S(1)}, bf16[192,128]{1,0:T(8,128)(2,1)S(1)}, u32[]{:S(2)}, u32[]{:S(2)}) collective-permute-start(bf16[192,128]{1,0:T(8,128)(2,1)S(1)} %bitcast.1085), channel_id=1, source_target_pairs={{0,24},{8,32},{16,40},{24,48},{32,56},{40,64},{48,72},{56,80},{64,... | collective-permute-start | bytes 147464 | tf_op jit(solution)/shard_map/ppermute | solution.py:34
  304.6 15.2 %all-to-all-start.4 = ((bf16[24,8,1024]{2,0,1:T(8,128)(2,1)}), bf16[24,8,1024]{2,0,1:T(8,128)(2,1)}, u32[]{:S(2)}, u32[]{:S(2)}) async-start(bf16[24,8,1024]{2,0,1:T(8,128)(2,1)} %bitcast.1044), calls=%async_computation.4 | async-start | bytes 786432 | tf_op jit(solution)/shard_map/all_to_all | solution.py:91
  311.6 94.9 %collective-permute-start.12 = (bf16[192,1024]{1,0:T(8,128)(2,1)}, bf16[192,1024]{1,0:T(8,128)(2,1)}, u32[]{:S(2)}, u32[]{:S(2)}) collective-permute-start(bf16[192,1024]{1,0:T(8,128)(2,1)} %bitcast.310), channel_id=1, source_target_pairs={{8,0},{16,8},{24,16},{32,24},{40,32},{48,40},{56,48},{64,56},{72,6... | collective-permute-start | bytes 1179656 | tf_op jit(solution)/shard_map/ppermute | solution.py:34
  312.9 96.3 %collective-permute-start.16 = (bf16[192,1024]{1,0:T(8,128)(2,1)}, bf16[192,1024]{1,0:T(8,128)(2,1)}, u32[]{:S(2)}, u32[]{:S(2)}) collective-permute-start(bf16[192,1024]{1,0:T(8,128)(2,1)} %bitcast.310), channel_id=1, source_target_pairs={{16,0},{24,8},{32,16},{40,24},{48,32},{56,40},{64,48},{72,56},{80,... | collective-permute-start | bytes 1179656 | tf_op jit(solution)/shard_map/ppermute | solution.py:34
  322.2 85.8 %collective-permute-start.14 = (bf16[192,1024]{1,0:T(8,128)(2,1)}, bf16[192,1024]{1,0:T(8,128)(2,1)}, u32[]{:S(2)}, u32[]{:S(2)}) collective-permute-start(bf16[192,1024]{1,0:T(8,128)(2,1)} %bitcast.312), channel_id=1, source_target_pairs={{8,0},{16,8},{24,16},{32,24},{40,32},{48,40},{56,48},{64,56},{72,6... | collective-permute-start | bytes 1179656 | tf_op jit(solution)/shard_map/ppermute | solution.py:34
  326.3 84.2 %all-to-all-start.5 = ((bf16[8,24,1024]{2,1,0:T(8,128)(2,1)}), bf16[8,24,1024]{2,1,0:T(8,128)(2,1)}, u32[]{:S(2)}, u32[]{:S(2)}) async-start(bf16[8,24,1024]{2,1,0:T(8,128)(2,1)} %all_to_all.124), calls=%async_computation.5 | async-start | bytes 786432 | tf_op jit(solution)/shard_map/all_to_all | solution.py:255
  331.2 11.6 %collective-permute-start.11 = (f32[192]{0:T(256)S(1)}, f32[192]{0:T(256)S(1)}, u32[]{:S(2)}, u32[]{:S(2)}) collective-permute-start(f32[192]{0:T(256)S(1)} %get-tuple-element.1377), channel_id=1, source_target_pairs={{8,0},{16,8},{24,16},{32,24},{40,32},{48,40},{56,48},{64,56},{72,6... | collective-permute-start | bytes 2312 | tf_op jit(solution)/shard_map/ppermute | solution.py:34
  332.4 17.7 %collective-permute-start.10 = (f32[192]{0:T(256)S(1)}, f32[192]{0:T(256)S(1)}, u32[]{:S(2)}, u32[]{:S(2)}) collective-permute-start(f32[192]{0:T(256)S(1)} %get-tuple-element.1377), channel_id=1, source_target_pairs={{16,0},{24,8},{32,16},{40,24},{48,32},{56,40},{64,48},{72,56},{80,... | collective-permute-start | bytes 2312 | tf_op jit(solution)/shard_map/ppermute | solution.py:34
  342.8 15.4 %collective-permute-start.9 = (f32[192]{0:T(256)S(1)}, f32[192]{0:T(256)S(1)}, u32[]{:S(2)}, u32[]{:S(2)}) collective-permute-start(f32[192]{0:T(256)S(1)} %get-tuple-element.1377), channel_id=1, source_target_pairs={{24,0},{32,8},{40,16},{48,24},{56,32},{64,40},{72,48},{80,56},{88,... | collective-permute-start | bytes 2312 | tf_op jit(solution)/shard_map/ppermute | solution.py:34
  350.1 27.3 %collective-permute-start.8 = (f32[192]{0:T(256)S(1)}, f32[192]{0:T(256)S(1)}, u32[]{:S(2)}, u32[]{:S(2)}) collective-permute-start(f32[192]{0:T(256)S(1)} %get-tuple-element.1377), channel_id=1, source_target_pairs={{32,0},{40,8},{48,16},{56,24},{64,32},{72,40},{80,48},{88,56},{96,... | collective-permute-start | bytes 2312 | tf_op jit(solution)/shard_map/ppermute | solution.py:34
  358.3 20.5 %collective-permute-start.15 = (f32[1,8,192]{1,2,0:T(8,128)S(1)}, f32[1,8,192]{1,2,0:T(8,128)S(1)}, u32[]{:S(2)}, u32[]{:S(2)}) collective-permute-start(f32[1,8,192]{1,2,0:T(8,128)S(1)} %bitcast.1078), channel_id=1, source_target_pairs={{8,0},{16,8},{24,16},{32,24},{40,32},{48,40},{56,48},{64,56},{72,6... | collective-permute-start | bytes 18440 | tf_op jit(solution)/shard_map/ppermute | solution.py:34
  387.3 9.7 %collective-permute-start.23 = (f32[1,8,192]{1,2,0:T(8,128)S(1)}, f32[1,8,192]{1,2,0:T(8,128)S(1)}, u32[]{:S(2)}, u32[]{:S(2)}) collective-permute-start(f32[1,8,192]{1,2,0:T(8,128)S(1)} %bitcast.1080), channel_id=1, source_target_pairs={{24,0},{32,8},{40,16},{48,24},{56,32},{64,40},{72,48},{80,56},{88,... | collective-permute-start | bytes 18440 | tf_op jit(solution)/shard_map/ppermute | solution.py:34
  389.1 10.1 %collective-permute-start.21 = (f32[1,8,192]{2,1,0:T(8,128)S(1)}, f32[1,8,192]{2,1,0:T(8,128)S(1)}, u32[]{:S(2)}, u32[]{:S(2)}) collective-permute-start(f32[1,8,192]{2,1,0:T(8,128)S(1)} %log_add_fusion), channel_id=1, source_target_pairs={{24,0},{32,8},{40,16},{48,24},{56,32},{64,40},{72,48},{80,56},{88,... | collective-permute-start | bytes 18440 | tf_op jit(solution)/shard_map/ppermute | solution.py:34
  397.0 23.2 %collective-permute-start.18 = (bf16[192,1024]{1,0:T(8,128)(2,1)}, bf16[192,1024]{1,0:T(8,128)(2,1)}, u32[]{:S(2)}, u32[]{:S(2)}) collective-permute-start(bf16[192,1024]{1,0:T(8,128)(2,1)} %bitcast.312), channel_id=1, source_target_pairs={{16,0},{24,8},{32,16},{40,24},{48,32},{56,40},{64,48},{72,56},{80,... | collective-permute-start | bytes 1179656 | tf_op jit(solution)/shard_map/ppermute | solution.py:34
  399.2 40.6 %collective-permute-start.20 = (bf16[192,1024]{1,0:T(8,128)(2,1)}, bf16[192,1024]{1,0:T(8,128)(2,1)}, u32[]{:S(2)}, u32[]{:S(2)}) collective-permute-start(bf16[192,1024]{1,0:T(8,128)(2,1)} %bitcast.310), channel_id=1, source_target_pairs={{24,0},{32,8},{40,16},{48,24},{56,32},{64,40},{72,48},{80,56},{88,... | collective-permute-start | bytes 1179656 | tf_op jit(solution)/shard_map/ppermute | solution.py:34
  406.5 74.3 %collective-permute-start.22 = (bf16[192,1024]{1,0:T(8,128)(2,1)}, bf16[192,1024]{1,0:T(8,128)(2,1)}, u32[]{:S(2)}, u32[]{:S(2)}) collective-permute-start(bf16[192,1024]{1,0:T(8,128)(2,1)} %bitcast.312), channel_id=1, source_target_pairs={{24,0},{32,8},{40,16},{48,24},{56,32},{64,40},{72,48},{80,56},{88,... | collective-permute-start | bytes 1179656 | tf_op jit(solution)/shard_map/ppermute | solution.py:34
  408.0 139.8 %collective-permute-start.24 = (bf16[192,1024]{1,0:T(8,128)(2,1)}, bf16[192,1024]{1,0:T(8,128)(2,1)}, u32[]{:S(2)}, u32[]{:S(2)}) collective-permute-start(bf16[192,1024]{1,0:T(8,128)(2,1)} %bitcast.310), channel_id=1, source_target_pairs={{32,0},{40,8},{48,16},{56,24},{64,32},{72,40},{80,48},{88,56},{96,... | collective-permute-start | bytes 1179656 | tf_op jit(solution)/shard_map/ppermute | solution.py:34
  409.3 138.5 %collective-permute-start.26 = (bf16[192,1024]{1,0:T(8,128)(2,1)}, bf16[192,1024]{1,0:T(8,128)(2,1)}, u32[]{:S(2)}, u32[]{:S(2)}) collective-permute-start(bf16[192,1024]{1,0:T(8,128)(2,1)} %bitcast.312), channel_id=1, source_target_pairs={{32,0},{40,8},{48,16},{56,24},{64,32},{72,40},{80,48},{88,56},{96,... | collective-permute-start | bytes 1179656 | tf_op jit(solution)/shard_map/ppermute | solution.py:34
  410.6 137.8 %all-to-all-start.3 = ((bf16[8,24,1024]{2,1,0:T(8,128)(2,1)}), bf16[8,24,1024]{2,1,0:T(8,128)(2,1)}, u32[]{:S(2)}, u32[]{:S(2)}) async-start(bf16[8,24,1024]{2,1,0:T(8,128)(2,1)} %all_to_all.117), calls=%async_computation.3 | async-start | bytes 786432 | tf_op jit(solution)/shard_map/all_to_all | solution.py:254
  420.2 127.4 %collective-permute-start.27 = (f32[1,8,192]{1,2,0:T(8,128)S(1)}, f32[1,8,192]{1,2,0:T(8,128)S(1)}, u32[]{:S(2)}, u32[]{:S(2)}) collective-permute-start(f32[1,8,192]{1,2,0:T(8,128)S(1)} %bitcast.1081), channel_id=1, source_target_pairs={{32,0},{40,8},{48,16},{56,24},{64,32},{72,40},{80,48},{88,56},{96,... | collective-permute-start | bytes 18440 | tf_op jit(solution)/shard_map/ppermute | solution.py:34
  439.8 107.9 %collective-permute-start.25 = (f32[1,8,192]{2,1,0:T(8,128)S(1)}, f32[1,8,192]{2,1,0:T(8,128)S(1)}, u32[]{:S(2)}, u32[]{:S(2)}) collective-permute-start(f32[1,8,192]{2,1,0:T(8,128)S(1)} %log_add_fusion), channel_id=1, source_target_pairs={{32,0},{40,8},{48,16},{56,24},{64,32},{72,40},{80,48},{88,56},{96,... | collective-permute-start | bytes 18440 | tf_op jit(solution)/shard_map/ppermute | solution.py:34
  548.4 12.7 %all-to-all-start.7 = ((bf16[8,24,128]{2,1,0:T(8,128)(2,1)}), bf16[8,24,128]{2,1,0:T(8,128)(2,1)S(1)}, u32[]{:S(2)}, u32[]{:S(2)}) async-start(bf16[8,24,128]{2,1,0:T(8,128)(2,1)} %bitcast.324), calls=%async_computation.7 | async-start | bytes 98304 | tf_op jit(solution)/shard_map/all_to_all | solution.py:257
  561.1 9.0 %all-to-all-start.6 = ((bf16[8,24,128]{2,1,0:T(8,128)(2,1)}), bf16[8,24,128]{2,1,0:T(8,128)(2,1)S(1)}, u32[]{:S(2)}, u32[]{:S(2)}) async-start(bf16[8,24,128]{2,1,0:T(8,128)(2,1)} %bitcast.322), calls=%async_computation.6 | async-start | bytes 98304 | tf_op jit(solution)/shard_map/all_to_all | solution.py:256
  (15 other events, 477.2 us)
where the time goes:
time: 580 us; the launch traced here: 571 us
  waiting for transfers between devices  183 us (32%)
  loops' own time  166 us (29%)
  starting transfers between devices  115 us (20%)
  local copies, waits for them, and re-layouts  60.6 us (10%)
  blocking collectives  24.8 us (4%)
  other arithmetic  7.68 us (1%)
  matrix products  7.12 us (1%)
  between operations  6.71 us (1%)
    ppermute x28, waiting for transfers between devices, shifted(): return lax.ppermute(block, axis, route)  175 us
    another operation x1, loops' own time, prefix(): return lax.fori_loop(0, length, step, start)  166 us
    ppermute x28, starting transfers between devices, shifted(): return lax.ppermute(block, axis, route)  56.1 us
    dynamic_slice x64, local copies, waits for them, and re-layouts, step(): new = combine(before, jax.tree.map(lambda part: part[k], everything))  41.8 us
    unnamed x1, blocking collectives  24.8 us
  transfers between devices with their start and end apart: 36, of which 17 were waited for; matrix products, arithmetic and copies ran while one was open for 12% of the time, Pallas kernels for 0%

commit v1 on v0

v1 whole, which is shorter than its diff:
```python
import math

import jax
import jax.numpy as jnp
from jax import lax
from jax.experimental import pallas as pl
from jax.experimental.pallas import tpu as pltpu
from jax.sharding import PartitionSpec as P

HEADS = 64
KV_HEADS = 8
HEAD_DIM = 128
GROUPS = HEADS // KV_HEADS
SPAN = 4
BLOCKS = SPAN + 1
TP = 8
PART = 24
TOK = TP * PART
WIDE = GROUPS * HEAD_DIM
PAIRS = GROUPS // 2
ROWS = 2 * TOK
SCALE = 1.0 / math.sqrt(HEAD_DIM)
SCALE_LOG2 = SCALE * math.log2(math.e)
MASKED = -1e30
MESH = pl.DeviceIdType.MESH
F32 = jnp.float32
BF16 = jnp.bfloat16

NT = (((1,), (1,)), ((), ()))
NN = (((1,), (0,)), ((), ()))


def dot(a, b, dims=NN):
    return lax.dot_general(a, b, dims, preferred_element_type=F32)


def landed(ref, sem):
    pltpu.make_async_copy(ref, ref, sem).wait()


def column_of(row):
    i = lax.broadcasted_iota(jnp.int32, (TOK, TOK), 0)
    j = lax.broadcasted_iota(jnp.int32, (TOK, TOK), 1)
    return jnp.sum(jnp.where(i == j, row, 0.0), axis=1, keepdims=True)


def kernel(
    q_in, k_in, v_in, g_in, seg_in,
    o_out, dq_out, dk_out, dv_out,
    qb, gb, kb, vb,
    kx, vx, sx, vt, kt, bias,
    qp, gp, scores, dprobs, probs, dscores,
    ob, dqb, dkb, dvb,
    tk, tv, rk, rv,
    local_sem, in_send, in_recv, hop_send, hop_recv, back_send, back_recv, out_send, out_recv,
):
    ctx = lax.axis_index("ctx")
    me = lax.axis_index("tp")
    n_ctx = lax.axis_size("ctx")
    after = lax.rem(ctx + 1, n_ctx)
    before = lax.rem(ctx + n_ctx - 1, n_ctx)

    barrier = pltpu.get_barrier_semaphore()

    def greet(j, carry):
        pl.semaphore_signal(
            barrier, inc=1, device_id=(ctx, lax.rem(me + j, TP)), device_id_type=MESH
        )
        return carry

    lax.fori_loop(1, TP, greet, 0)
    pl.semaphore_signal(barrier, inc=1, device_id=(after, me), device_id_type=MESH)
    pl.semaphore_signal(barrier, inc=1, device_id=(before, me), device_id_type=MESH)
    pl.semaphore_wait(barrier, TP + 1)

    def columns(owner, width):
        return pl.ds(pl.multiple_of(owner * width, width), width)

    def scatter(src, buf, width, n):
        def send(j, carry):
            peer = lax.rem(me + j, TP)
            pltpu.make_async_remote_copy(
                src_ref=src.at[:, columns(peer, width)],
                dst_ref=buf.at[me],
                send_sem=in_send.at[n],
                recv_sem=in_recv.at[n],
                device_id=(ctx, peer),
                device_id_type=MESH,
            ).start()
            return carry

        lax.fori_loop(1, TP, send, 0)
        pltpu.make_async_copy(src.at[:, columns(me, width)], buf.at[me], local_sem.at[n]).start()

    def gathered(buf, n):
        landed(buf.at[pl.ds(0, TP - 1)], in_recv.at[n])
        landed(buf.at[0], local_sem.at[n])

    scatter(k_in, kb, HEAD_DIM, 0)
    scatter(v_in, vb, HEAD_DIM, 1)
    scatter(q_in, qb, WIDE, 2)
    scatter(g_in, gb, WIDE, 3)

    def joined(buf, low):
        parts = [buf[r, :, low : low + HEAD_DIM].astype(F32) for r in range(TP)]
        return jnp.concatenate(parts, axis=0).astype(BF16)

    sx[0] = seg_in[...].astype(F32)

    def hop(buf, d, n):
        pltpu.make_async_remote_copy(
            src_ref=buf.at[d],
            dst_ref=buf.at[d + 1],
            send_sem=hop_send.at[n, d],
            recv_sem=hop_recv.at[n, d],
            device_id=(after, me),
            device_id_type=MESH,
        ).start()

    hop(sx, 0, 2)
    gathered(kb, 0)
    kx[0] = joined(kb, 0)
    hop(kx, 0, 0)
    gathered(vb, 1)
    vx[0] = joined(vb, 0)
    hop(vx, 0, 1)
    for d in range(1, BLOCKS):
        for buf, n in ((sx, 2), (kx, 0), (vx, 1)):
            landed(buf.at[d], hop_recv.at[n, d - 1])
            if d < SPAN:
                hop(buf, d, n)

    own = sx[0]
    own_wide = jnp.concatenate([own, own], axis=1)
    for d in range(BLOCKS):
        seen = column_of(sx[d]) == own_wide
        if d == 0:
            i = lax.broadcasted_iota(jnp.int32, (TOK, TOK), 0)
            j = lax.broadcasted_iota(jnp.int32, (TOK, TOK), 1)
            causal = jnp.where(i <= j, 0.0, MASKED)
            bias[d] = jnp.where(seen, jnp.concatenate([causal, causal], axis=1), MASKED)
        else:
            bias[d] = jnp.where(seen, 0.0, MASKED)
        kt[d] = kx[d].astype(F32).T.astype(BF16)
        vt[d] = vx[d].astype(F32).T.astype(BF16)

    gathered(qb, 2)
    for h in range(GROUPS):
        qp[h * TOK : (h + 1) * TOK, :] = joined(qb, h * HEAD_DIM)
    gathered(gb, 3)
    for h in range(GROUPS):
        gp[h * TOK : (h + 1) * TOK, :] = joined(gb, h * HEAD_DIM)

    def pair_step(hp, carry):
        rows = pl.ds(pl.multiple_of(hp * ROWS, ROWS), ROWS)
        q2 = qp[rows, :]
        g2 = gp[rows, :]
        top = None
        for d in range(BLOCKS):
            s = dot(kx[d], q2, NT) * SCALE_LOG2 + bias[d]
            scores[d] = s
            here = jnp.max(s, axis=0, keepdims=True)
            top = here if top is None else jnp.maximum(top, here)
        total = jnp.zeros_like(top)
        weighted = jnp.zeros_like(top)
        for d in range(BLOCKS):
            e = jnp.exp2(scores[d] - top)
            total += jnp.sum(e, axis=0, keepdims=True)
            dp = dot(vx[d], g2, NT)
            weighted += jnp.sum(e * dp, axis=0, keepdims=True)
            scores[d] = e
            dprobs[d] = dp
        inverse = 1.0 / total
        row_dot = weighted * inverse
        o_t = None
        dq_t = None
        for d in range(BLOCKS):
            p = scores[d] * inverse
            p_low = p.astype(BF16)
            ds = (p * (dprobs[d] - row_dot)).astype(BF16)
            probs[d, :, rows] = p_low
            dscores[d, :, rows] = ds
            o_d = dot(vt[d], p_low)
            dq_d = dot(kt[d], ds)
            o_t = o_d if o_t is None else o_t + o_d
            dq_t = dq_d if dq_t is None else dq_t + dq_d
        o = o_t.T
        dq = (dq_t * SCALE).T
        for i in range(2):
            lanes = pl.ds(pl.multiple_of((2 * hp + i) * HEAD_DIM, HEAD_DIM), HEAD_DIM)
            for r in range(TP):
                low = i * TOK + r * PART
                ob[r, :, lanes] = o[low : low + PART].astype(BF16)
                dqb[r, :, lanes] = dq[low : low + PART].astype(BF16)
        return carry

    lax.fori_loop(0, PAIRS, pair_step, 0)

    def give(buf, dst, width, n):
        def send(j, carry):
            peer = lax.rem(me + j, TP)
            pltpu.make_async_remote_copy(
                src_ref=buf.at[peer],
                dst_ref=dst.at[:, columns(me, width)],
                send_sem=out_send.at[n],
                recv_sem=out_recv.at[n],
                device_id=(ctx, peer),
                device_id_type=MESH,
            ).start()
            return carry

        lax.fori_loop(1, TP, send, 0)
        pltpu.make_async_copy(
            buf.at[me], dst.at[:, columns(me, width)], local_sem.at[4 + n]
        ).start()

    def back(src, dst, h, n):
        pltpu.make_async_remote_copy(
            src_ref=src.at[h],
            dst_ref=dst.at[h],
            send_sem=back_send.at[n, h],
            recv_sem=back_recv.at[n, h],
            device_id=(before, me),
            device_id_type=MESH,
        ).start()

    give(ob, o_out, WIDE, 0)
    give(dqb, dq_out, WIDE, 1)

    for h in range(BLOCKS):
        d = SPAN - h
        for n, (left, right, scaling, tx, rx) in enumerate(
            ((probs, gp, 1.0, tv, rv), (dscores, qp, SCALE, tk, rk))
        ):
            term = dot(left[d], right[...]) * scaling
            if h > 0:
                landed(rx.at[h - 1], back_recv.at[n, h - 1])
                term += rx[h - 1].astype(F32)
            if h < SPAN:
                tx[h] = term.astype(BF16)
                back(tx, rx, h, n)
            else:
                final = dvb if n == 0 else dkb
                for r in range(TP):
                    final[r] = term[r * PART : (r + 1) * PART].astype(BF16)
                if n == 0:
                    give(dvb, dv_out, HEAD_DIM, 2)
                else:
                    give(dkb, dk_out, HEAD_DIM, 3)

    for n, (buf, dst) in enumerate(((ob, o_out), (dqb, dq_out), (dvb, dv_out), (dkb, dk_out))):
        landed(buf.at[pl.ds(0, TP - 1)], out_recv.at[n])
        landed(buf.at[0], local_sem.at[4 + n])
        landed(buf.at[pl.ds(0, TP - 1)], out_send.at[n])
    for n, buf in enumerate((kb, vb, qb, gb)):
        landed(buf.at[pl.ds(0, TP - 1)], in_send.at[n])
    for d in range(SPAN):
        for n, buf in enumerate((kx, vx, sx)):
            landed(buf.at[d], hop_send.at[n, d])
        for n, buf in enumerate((tv, tk)):
            landed(buf.at[d], back_send.at[n, d])


def body(query_in, key_in, value_in, grad_out, segments):
    any_spec = pl.BlockSpec(memory_space=pl.ANY)
    vmem_spec = pl.BlockSpec(memory_space=pltpu.VMEM)
    sem = pltpu.SemaphoreType.DMA
    return pl.pallas_call(
        kernel,
        out_shape=(
            jax.ShapeDtypeStruct((PART, HEADS * HEAD_DIM), BF16),
            jax.ShapeDtypeStruct((PART, HEADS * HEAD_DIM), BF16),
            jax.ShapeDtypeStruct((PART, KV_HEADS * HEAD_DIM), BF16),
            jax.ShapeDtypeStruct((PART, KV_HEADS * HEAD_DIM), BF16),
        ),
        in_specs=[any_spec] * 4 + [vmem_spec],
        out_specs=(any_spec,) * 4,
        scratch_shapes=[
            pltpu.VMEM((TP, PART, WIDE), BF16),
            pltpu.VMEM((TP, PART, WIDE), BF16),
            pltpu.VMEM((TP, PART, HEAD_DIM), BF16),
            pltpu.VMEM((TP, PART, HEAD_DIM), BF16),
            pltpu.VMEM((BLOCKS, TOK, HEAD_DIM), BF16),
            pltpu.VMEM((BLOCKS, TOK, HEAD_DIM), BF16),
            pltpu.VMEM((BLOCKS, 1, TOK), F32),
            pltpu.VMEM((BLOCKS, HEAD_DIM, TOK), BF16),
            pltpu.VMEM((BLOCKS, HEAD_DIM, TOK), BF16),
            pltpu.VMEM((BLOCKS, TOK, ROWS), F32),
            pltpu.VMEM((GROUPS * TOK, HEAD_DIM), BF16),
            pltpu.VMEM((GROUPS * TOK, HEAD_DIM), BF16),
            pltpu.VMEM((BLOCKS, TOK, ROWS), F32),
            pltpu.VMEM((BLOCKS, TOK, ROWS), F32),
            pltpu.VMEM((BLOCKS, TOK, GROUPS * TOK), BF16),
            pltpu.VMEM((BLOCKS, TOK, GROUPS * TOK), BF16),
            pltpu.VMEM((TP, PART, WIDE), BF16),
            pltpu.VMEM((TP, PART, WIDE), BF16),
            pltpu.VMEM((TP, PART, HEAD_DIM), BF16),
            pltpu.VMEM((TP, PART, HEAD_DIM), BF16),
            pltpu.VMEM((SPAN, TOK, HEAD_DIM), BF16),
            pltpu.VMEM((SPAN, TOK, HEAD_DIM), BF16),
            pltpu.VMEM((SPAN, TOK, HEAD_DIM), BF16),
            pltpu.VMEM((SPAN, TOK, HEAD_DIM), BF16),
            sem((8,)),
            sem((4,)),
            sem((4,)),
            sem((3, SPAN)),
            sem((3, SPAN)),
            sem((2, SPAN)),
            sem((2, SPAN)),
            sem((4,)),
            sem((4,)),
        ],
        compiler_params=pltpu.CompilerParams(
            collective_id=0, has_side_effects=True, vmem_limit_bytes=48 * 1024 * 1024
        ),
    )(query_in, key_in, value_in, grad_out, segments.reshape(1, TOK))


def solution(mesh):
    split = P(("ctx", "tp"), None)
    return jax.shard_map(
        body,
        mesh=mesh,
        in_specs=(split, split, split, split, P("ctx")),
        out_specs=(split, split, split, split),
        check_vma=False,
    )
```

time: 580 us -> 68.2 us (0.12); the launches traced: 571 us -> 67.9 us
  waiting for transfers between devices: 183 us -> 0 us
  loops' own time: 166 us -> 0 us
  starting transfers between devices: 115 us -> 0 us
  Pallas kernels: 0 us -> 60.3 us
  local copies, waits for them, and re-layouts: 60.6 us -> 6.99 us
  blocking collectives: 24.8 us -> 0 us
  other arithmetic: 7.68 us -> 0 us
  matrix products: 7.12 us -> 0 us
  between operations: 6.71 us -> 0.65 us
    ppermute x28 -> x0, waiting for transfers between devices: 175 us -> none  [shifted(): return lax.ppermute(block, axis, route)]
    another operation x17 -> x0, loops' own time: 166 us -> none  [the longest x1 166 us: prefix(): return lax.fori_loop(0, length, step, start)]
    pallas_call x0 -> x1, Pallas kernels: none -> 60.3 us  [body(): pl.pallas_call(kernel, out_shape=(jax.ShapeDtypeStruct((PART, HEADS * HEA...]
    all_to_all x8 -> x0, starting transfers between devices: 58.9 us -> none  [the longest x1 10.1 us: body(): lax.all_to_all(key_in, 'tp', split_axis=1, concat_axis=0, tiled=True)]
    ppermute x28 -> x0, starting transfers between devices: 56.1 us -> none  [shifted(): return lax.ppermute(block, axis, route)]
    dynamic_slice x64 -> x0, local copies, waits for them, and re-layouts: 41.8 us -> none  [step(): new = combine(before, jax.tree.map(lambda part: part[k], everything))]
    unnamed x1 -> x0, blocking collectives: 24.8 us -> none
    all_to_all x10 -> x0, local copies, waits for them, and re-layouts: 11.2 us -> none  [the longest x2 2.68 us: body(): lax.all_to_all(query_flat, 'tp', split_axis=0, concat_axis=1, tiled=True)]
  transfers between devices with their start and end apart: 36 -> 0, of which waited for: 17 -> 0; matrix products, arithmetic and copies ran while one was open for 12% -> 0% of each run, Pallas kernels for 0% -> 0%
where the time goes in v1:
time: 68.2 us; the launch traced here: 67.9 us
  Pallas kernels  60.3 us (88%)
  local copies, waits for them, and re-layouts  6.99 us (10%)
    pallas_call x1, Pallas kernels, body(): pl.pallas_call(kernel, out_shape=(jax.ShapeDtypeStruct((PART, HEADS * HEA...  60.3 us
    unnamed x14, local copies, waits for them, and re-layouts  6.99 us

profile of v1, /device:TPU:1, one launch (start us, length us, event | category | flops | bytes accessed | tf_op | source)
XLA Modules:
  0.0 67.9 jit_solution(1439398200246756178)
XLA Ops:
  0.6 0.0 copy-start.4
  0.6 0.7 copy-done.4
  1.3 0.0 copy-start
  1.3 1.0 %copy-done = bf16[24,8192]{1,0:T(8,128)(2,1)S(1)} copy-done((bf16[24,8192]{1,0:T(8,128)(2,1)S(1)}, bf16[24,8192]{1,0:T(8,128)(2,1)}, u32[]{:S(2)}) %copy-start) | copy-done | bytes 393240
  2.3 0.0 copy-start.1
  2.3 1.0 %copy-done.1 = bf16[24,8192]{1,0:T(8,128)(2,1)S(1)} copy-done((bf16[24,8192]{1,0:T(8,128)(2,1)S(1)}, bf16[24,8192]{1,0:T(8,128)(2,1)}, u32[]{:S(2)}) %copy-start.1) | copy-done | bytes 393240
  3.3 0.0 copy-start.2
  3.3 0.8 %copy-done.2 = bf16[24,1024]{1,0:T(8,128)(2,1)S(1)} copy-done((bf16[24,1024]{1,0:T(8,128)(2,1)S(1)}, bf16[24,1024]{1,0:T(8,128)(2,1)}, u32[]{:S(2)}) %copy-start.2) | copy-done | bytes 49176
  4.1 0.0 copy-start.3
  4.1 0.8 %copy-done.3 = bf16[24,1024]{1,0:T(8,128)(2,1)S(1)} copy-done((bf16[24,1024]{1,0:T(8,128)(2,1)S(1)}, bf16[24,1024]{1,0:T(8,128)(2,1)}, u32[]{:S(2)}) %copy-start.3) | copy-done | bytes 49176
  4.9 60.3 %shard_map.84 = (bf16[24,8192]{1,0:T(8,128)(2,1)S(1)}, bf16[24,8192]{1,0:T(8,128)(2,1)S(1)}, bf16[24,1024]{1,0:T(8,128)(2,1)S(1)}, bf16[24,1024]{1,0:T(8,128)(2,1)S(1)}) custom-call(bf16[24,8192]{1,0:T(8,128)(2,1)S(1)} %copy-done, bf16[24,1024]{1,0:T(8,128)(2,1)S(1)} %copy-done.2, bf16[24,1024]{1,0:T(8,128)(2,1)S(1)} %copy-done.3, ...), custom_call_target="tpu_custom_call" | custom-call | tf_op jit(solution)/shard_map/pallas_call | solution.py:268
  65.2 0.7 %copy.13 = bf16[24,8192]{1,0:T(8,128)(2,1)} copy(bf16[24,8192]{1,0:T(8,128)(2,1)S(1)} %get-tuple-element.8) | data formatting | bytes 786432
  65.9 0.7 %copy.14 = bf16[24,8192]{1,0:T(8,128)(2,1)} copy(bf16[24,8192]{1,0:T(8,128)(2,1)S(1)} %get-tuple-element.9) | data formatting | bytes 786432
  66.7 0.6 copy.15
  67.3 0.6 copy.16
Async XLA Ops:
  0.6 0.7 %copy-start.4 = (s32[192]{0:T(256)S(1)}, s32[192]{0:T(256)}, u32[]{:S(2)}) copy-start(s32[192]{0:T(256)} %param.9) | copy-start | bytes 2308
  1.3 1.0 %copy-start = (bf16[24,8192]{1,0:T(8,128)(2,1)S(1)}, bf16[24,8192]{1,0:T(8,128)(2,1)}, u32[]{:S(2)}) copy-start(bf16[24,8192]{1,0:T(8,128)(2,1)} %q_in.1) | copy-start | bytes 1179652
  2.3 1.0 %copy-start.1 = (bf16[24,8192]{1,0:T(8,128)(2,1)S(1)}, bf16[24,8192]{1,0:T(8,128)(2,1)}, u32[]{:S(2)}) copy-start(bf16[24,8192]{1,0:T(8,128)(2,1)} %g_in.1) | copy-start | bytes 1179652
  3.3 0.8 %copy-start.2 = (bf16[24,1024]{1,0:T(8,128)(2,1)S(1)}, bf16[24,1024]{1,0:T(8,128)(2,1)}, u32[]{:S(2)}) copy-start(bf16[24,1024]{1,0:T(8,128)(2,1)} %k_in.1) | copy-start | bytes 147460
  4.1 0.8 %copy-start.3 = (bf16[24,1024]{1,0:T(8,128)(2,1)S(1)}, bf16[24,1024]{1,0:T(8,128)(2,1)}, u32[]{:S(2)}) copy-start(bf16[24,1024]{1,0:T(8,128)(2,1)} %v_in.1) | copy-start | bytes 147460

commit v2 on v1

v2 whole, which is shorter than its diff:
```python
import math

import jax
import jax.numpy as jnp
from jax import lax
from jax.experimental import pallas as pl
from jax.experimental.pallas import tpu as pltpu
from jax.sharding import PartitionSpec as P

HEADS = 64
KV_HEADS = 8
HEAD_DIM = 128
GROUPS = HEADS // KV_HEADS
SPAN = 4
BLOCKS = SPAN + 1
TP = 8
PART = 24
TOK = TP * PART
WIDE = GROUPS * HEAD_DIM
ALL_ROWS = GROUPS * TOK
PAIR = 2 * TOK
HEAD_ROWS = 16
HALF = TOK // 2
CHUNKS = TP // 2
SCALE = 1.0 / math.sqrt(HEAD_DIM)
SCALE_LOG2 = SCALE * math.log2(math.e)
MASKED = -1e30
MESH = pl.DeviceIdType.MESH
F32 = jnp.float32
BF16 = jnp.bfloat16

NT = (((1,), (1,)), ((), ()))
NN = (((1,), (0,)), ((), ()))

CUTS = ((0, HALF), (HALF, HALF))


def dot(a, b, dims=NN):
    return lax.dot_general(a, b, dims, preferred_element_type=F32)


def landed(ref, sem):
    pltpu.make_async_copy(ref, ref, sem).wait()


def column_of(row):
    i = lax.broadcasted_iota(jnp.int32, (TOK, TOK), 0)
    j = lax.broadcasted_iota(jnp.int32, (TOK, TOK), 1)
    return jnp.sum(jnp.where(i == j, row, 0.0), axis=1, keepdims=True)


def kernel(
    q_in, k_in, v_in, g_in, seg_in,
    o_out, dq_out, dk_out, dv_out,
    qs, gs, ks, vs, qb, gb, kc, vc, sg,
    kx, vx, bias, qp, gp,
    ex, dpx, tops, sums, dots, factors,
    pb, db, terms,
    ob, dqb, near, far, near_in, far_in,
    tx, rx,
    seg_v, load_sem, local_sem, in_send, in_recv, hop_send, hop_recv, back_send, back_recv,
    out_send, out_recv, end_send, end_recv,
):
    ctx = lax.axis_index("ctx")
    me = lax.axis_index("tp")
    n_ctx = lax.axis_size("ctx")
    after = lax.rem(ctx + 1, n_ctx)
    before = lax.rem(ctx + n_ctx - 1, n_ctx)

    loads = [
        pltpu.make_async_copy(src, dst, load_sem.at[n])
        for n, (src, dst) in enumerate(((k_in, ks), (v_in, vs), (q_in, qs), (g_in, gs), (seg_in, seg_v)))
    ]
    for load in loads:
        load.start()

    barrier = pltpu.get_barrier_semaphore()

    def greet(j, carry):
        peer = lax.rem(me + j, TP)
        pl.semaphore_signal(barrier, inc=1, device_id=(after, peer), device_id_type=MESH)
        pl.semaphore_signal(barrier, inc=1, device_id=(before, peer), device_id_type=MESH)
        return carry

    def greet_near(j, carry):
        peer = lax.rem(me + j, TP)
        pl.semaphore_signal(barrier, inc=1, device_id=(ctx, peer), device_id_type=MESH)
        return carry

    lax.fori_loop(0, TP, greet, 0)
    lax.fori_loop(1, TP, greet_near, 0)
    pl.semaphore_wait(barrier, 3 * TP - 1)

    def columns(owner, width):
        return pl.ds(pl.multiple_of(owner * width, width), width)

    def scatter(src, buf, width, n):
        def send(j, carry):
            peer = lax.rem(me + j, TP)
            pltpu.make_async_remote_copy(
                src_ref=src.at[:, columns(peer, width)],
                dst_ref=buf.at[me],
                send_sem=in_send.at[n],
                recv_sem=in_recv.at[n],
                device_id=(ctx, peer),
                device_id_type=MESH,
            ).start()
            return carry

        lax.fori_loop(1, TP, send, 0)
        pltpu.make_async_copy(src.at[:, columns(me, width)], buf.at[me], local_sem.at[n]).start()

    def scatter_on(src, buf, n):
        def send(j, carry):
            peer = lax.rem(me + j, TP)
            pltpu.make_async_remote_copy(
                src_ref=src.at[:, columns(peer, HEAD_DIM)],
                dst_ref=buf.at[1, me],
                send_sem=in_send.at[n],
                recv_sem=in_recv.at[n],
                device_id=(after, peer),
                device_id_type=MESH,
            ).start()
            return carry

        lax.fori_loop(0, TP, send, 0)

    def gathered(buf, n):
        landed(buf.at[pl.ds(0, TP - 1)], in_recv.at[n])
        landed(buf.at[0], local_sem.at[n])

    def joined(buf, low):
        parts = [buf[r, :, low : low + HEAD_DIM].astype(F32) for r in range(TP)]
        return jnp.concatenate(parts, axis=0).astype(BF16)

    def pass_on(src, dst, n, d):
        pltpu.make_async_remote_copy(
            src_ref=src,
            dst_ref=dst,
            send_sem=hop_send.at[n, d],
            recv_sem=hop_recv.at[n, d],
            device_id=(after, me),
            device_id_type=MESH,
        ).start()

    def hop_ids(d):
        if d > 0:
            landed(sg.at[d], hop_recv.at[4, d - 1])
        if d < SPAN:
            pass_on(sg.at[d], sg.at[d + 1], 4, d)

    def hop(buf, d, n):
        if d == 1:
            landed(buf.at[1], in_recv.at[4 + n])
        for c in range(2):
            part = pl.ds(c * CHUNKS, CHUNKS)
            if d > 1:
                landed(buf.at[d, part], hop_recv.at[2 * n + c, d - 1])
            if d < SPAN:
                pass_on(buf.at[d, part], buf.at[d + 1, part], 2 * n + c, d)

    def hop_keys(d):
        hop_ids(d)
        hop(kc, d, 0)

    def hop_values(d):
        hop(vc, d, 1)

    def ids_of(d):
        rows = sg[d].astype(F32)
        return jnp.concatenate([rows[0:1], rows[1:2, : TOK - 128]], axis=1)

    def make_bias(d):
        own = ids_of(0)
        seen = column_of(ids_of(d)) == jnp.concatenate([own, own], axis=1)
        if d == 0:
            i = lax.broadcasted_iota(jnp.int32, (TOK, TOK), 0)
            j = lax.broadcasted_iota(jnp.int32, (TOK, TOK), 1)
            causal = jnp.where(i <= j, 0.0, MASKED)
            bias[d] = jnp.where(seen, jnp.concatenate([causal, causal], axis=1), MASKED)
        else:
            bias[d] = jnp.where(seen, 0.0, MASKED)

    tiles = [slice(c * 128, (c + 1) * 128) for c in range(ALL_ROWS // 128)]
    bias_tiles = [slice((c % 3) * 128, (c % 3 + 1) * 128) for c in range(ALL_ROWS // 128)]

    def keys(d):
        return kx[d]

    def score(d):
        make_bias(d)
        kx[d] = joined(kc.at[d], 0)
        s = dot(keys(d), qp[...], NT)
        for lanes, cover in zip(tiles, bias_tiles):
            x = s[:, lanes] * SCALE_LOG2 + bias[d, :, cover]
            top = jnp.max(x, axis=0, keepdims=True)
            e = jnp.exp2(x - top)
            ex[d, :, lanes] = e
            tops[d, :, lanes] = top
            sums[d, :, lanes] = jnp.sum(e, axis=0, keepdims=True)

    def dprob(d):
        vx[d] = joined(vc.at[d], 0)
        t = dot(vx[d], gp[...], NT)
        for lanes in tiles:
            dp = t[:, lanes]
            dpx[d, :, lanes] = dp
            dots[d, :, lanes] = jnp.sum(ex[d, :, lanes] * dp, axis=0, keepdims=True)

    def combine():
        top = tops[0]
        for d in range(1, BLOCKS):
            top = jnp.maximum(top, tops[d])
        shares = [jnp.exp2(tops[d] - top) for d in range(BLOCKS)]
        inverse = 1.0 / sum(shares[d] * sums[d] for d in range(BLOCKS))
        for d in range(BLOCKS):
            factors[d] = shares[d] * inverse

    def combine_dots():
        factors[BLOCKS] = sum(factors[d] * dots[d] for d in range(BLOCKS))

    def weigh(d):
        for lanes in tiles:
            pb[d, :, lanes] = (ex[d, :, lanes] * factors[d, :, lanes]).astype(BF16)

    def weigh_keys(d):
        for lanes in tiles:
            p = ex[d, :, lanes] * factors[d, :, lanes]
            db[d, :, lanes] = (p * (dpx[d, :, lanes] - factors[BLOCKS, :, lanes])).astype(BF16)

    def value_term(d):
        terms[0, d] = dot(pb[d], gp[...])

    def key_term(d):
        terms[1, d] = dot(db[d], qp[...]) * SCALE

    def back(h, n):
        d = SPAN - h
        for c, (low, size) in enumerate(CUTS):
            rows = pl.ds(low, size)
            term = terms[n, d, rows]
            if h > 0:
                landed(rx.at[n, h - 1, rows], back_recv.at[2 * n + c, h - 1])
                term += rx[n, h - 1, rows].astype(F32)
            if h < SPAN - 1:
                tx[n, h, rows] = term.astype(BF16)
                pltpu.make_async_remote_copy(
                    src_ref=tx.at[n, h, rows],
                    dst_ref=rx.at[n, h, rows],
                    send_sem=back_send.at[2 * n + c, h],
                    recv_sem=back_recv.at[2 * n + c, h],
                    device_id=(before, me),
                    device_id_type=MESH,
                ).start()
            else:
                for r in range(CHUNKS):
                    far[n, c * CHUNKS + r] = term[r * PART : (r + 1) * PART].astype(BF16)

                def send(j, carry):
                    pltpu.make_async_remote_copy(
                        src_ref=far.at[n, j],
                        dst_ref=far_in.at[n, me],
                        send_sem=end_send.at[n],
                        recv_sem=end_recv.at[n],
                        device_id=(before, j),
                        device_id_type=MESH,
                    ).start()
                    return carry

                lax.fori_loop(c * CHUNKS, (c + 1) * CHUNKS, send, 0)

    def own_terms(n):
        for r in range(TP):
            near[n, r] = terms[n, 0, r * PART : (r + 1) * PART].astype(BF16)

        def send(j, carry):
            peer = lax.rem(me + j, TP)
            pltpu.make_async_remote_copy(
                src_ref=near.at[n, peer],
                dst_ref=near_in.at[n, me],
                send_sem=out_send.at[2 + n],
                recv_sem=out_recv.at[2 + n],
                device_id=(ctx, peer),
                device_id_type=MESH,
            ).start()
            return carry

        lax.fori_loop(1, TP, send, 0)
        pltpu.make_async_copy(near.at[n, me], near_in.at[n, me], local_sem.at[6 + n]).start()

    def close(n, dst):
        landed(near_in.at[n, pl.ds(0, TP - 1)], out_recv.at[2 + n])
        landed(near_in.at[n, 0], local_sem.at[6 + n])
        landed(far_in.at[n], end_recv.at[n])
        for h in range(TP):
            total = near_in[n, h].astype(F32) + far_in[n, h].astype(F32)
            dst[:, h * HEAD_DIM : (h + 1) * HEAD_DIM] = total.astype(BF16)

    def give(buf, dst, width, n):
        def send(j, carry):
            peer = lax.rem(me + j, TP)
            pltpu.make_async_remote_copy(
                src_ref=buf.at[peer],
                dst_ref=dst.at[:, columns(me, width)],
                send_sem=out_send.at[n],
                recv_sem=out_recv.at[n],
                device_id=(ctx, peer),
                device_id_type=MESH,
            ).start()
            return carry

        lax.fori_loop(1, TP, send, 0)
        pltpu.make_async_copy(
            buf.at[me], dst.at[:, columns(me, width)], local_sem.at[4 + n]
        ).start()

    def product(parts, low, scaling, buf, dst, n):
        for h in range(0, GROUPS, 2):
            lanes = slice(h * TOK, h * TOK + PAIR)
            total = None
            for d in range(BLOCKS):
                one = dot(low(d), parts[d, :, lanes])
                total = one if total is None else total + one
            both = (total * scaling).T
            for i in range(2):
                for r in range(TP):
                    start = i * TOK + r * PART
                    buf[r, :, (h + i) * HEAD_DIM : (h + i + 1) * HEAD_DIM] = both[
                        start : start + PART
                    ].astype(BF16)
        give(buf, dst, WIDE, n)

    def drain():
        for n, (buf, dst) in enumerate(((ob, o_out), (dqb, dq_out))):
            landed(buf.at[pl.ds(0, TP - 1)], out_recv.at[n])
            landed(buf.at[0], local_sem.at[4 + n])
            landed(buf.at[pl.ds(0, TP - 1)], out_send.at[n])
        for n, buf in enumerate((kc.at[0], vc.at[0], qb, gb)):
            landed(buf.at[pl.ds(0, TP - 1)], in_send.at[n])
        for n, buf in enumerate((kc, vc)):
            landed(buf.at[1], in_send.at[4 + n])
        landed(sg.at[0], hop_send.at[4, 0])
        for d in range(1, SPAN):
            landed(sg.at[d], hop_send.at[4, d])
            for c in range(2):
                part = pl.ds(c * CHUNKS, CHUNKS)
                landed(kc.at[d, part], hop_send.at[c, d])
                landed(vc.at[d, part], hop_send.at[2 + c, d])
        for n in range(2):
            for h in range(SPAN - 1):
                for c, (low, size) in enumerate(CUTS):
                    landed(tx.at[n, h, pl.ds(low, size)], back_send.at[2 * n + c, h])
            landed(near.at[n, pl.ds(0, TP - 1)], out_send.at[2 + n])
            landed(far.at[n], end_send.at[n])

    loads[4].wait()
    ids = seg_v[...].astype(F32)
    late_ids = jnp.concatenate([ids[:, 128:TOK], jnp.zeros((1, 256 - TOK), F32)], axis=1)
    place = lax.broadcasted_iota(jnp.int32, (HEAD_ROWS, 128), 0)
    head = jnp.where(place == 0, ids[:, :128], jnp.where(place == 1, late_ids, 0.0))
    sg[0] = head.astype(BF16)
    loads[0].wait()
    loads[1].wait()
    scatter_on(ks, kc, 4)
    hop_ids(0)
    scatter(ks, kc.at[0], HEAD_DIM, 0)
    scatter_on(vs, vc, 5)
    scatter(vs, vc.at[0], HEAD_DIM, 1)
    loads[2].wait()
    scatter(qs, qb, WIDE, 2)
    hop_keys(1)
    hop_values(1)
    loads[3].wait()
    scatter(gs, gb, WIDE, 3)
    hop_keys(2)
    hop_values(2)
    gathered(qb, 2)
    for h in range(GROUPS):
        qp[h * TOK : (h + 1) * TOK, :] = joined(qb, h * HEAD_DIM)
    gathered(kc.at[0], 0)
    score(0)
    hop_keys(3)
    score(1)
    hop_values(3)
    score(2)
    score(3)
    gathered(gb, 3)
    for h in range(GROUPS):
        gp[h * TOK : (h + 1) * TOK, :] = joined(gb, h * HEAD_DIM)
    gathered(vc.at[0], 1)
    dprob(0)
    dprob(1)
    dprob(2)
    dprob(3)
    hop_keys(4)
    score(4)
    combine()
    weigh(4)
    value_term(4)
    back(0, 0)
    weigh(3)
    weigh(2)
    hop_values(4)
    dprob(4)
    combine_dots()
    weigh_keys(4)
    key_term(4)
    back(0, 1)
    weigh(1)
    weigh(0)
    product(pb, lambda d: vx[d].astype(F32).T.astype(BF16), 1.0, ob, o_out, 0)
    value_term(3)
    back(1, 0)
    weigh_keys(3)
    key_term(3)
    back(1, 1)
    weigh_keys(2)
    weigh_keys(1)
    weigh_keys(0)
    product(db, lambda d: keys(d).astype(F32).T.astype(BF16), SCALE, dqb, dq_out, 1)
    value_term(2)
    back(2, 0)
    key_term(2)
    back(2, 1)
    value_term(0)
    own_terms(0)
    key_term(0)
    own_terms(1)
    value_term(1)
    back(3, 0)
    key_term(1)
    back(3, 1)
    close(0, dv_out)
    close(1, dk_out)
    drain()


def deliver(o, dq, dk, dv, o_out, dq_out, dk_out, dv_out, sems):
    copies = [
        pltpu.make_async_copy(src, dst, sems.at[n])
        for n, (src, dst) in enumerate(((o, o_out), (dq, dq_out), (dk, dk_out), (dv, dv_out)))
    ]
    for copy in copies:
        copy.start()
    for copy in copies:
        copy.wait()


def body(query_in, key_in, value_in, grad_out, segments):
    hbm_spec = pl.BlockSpec(memory_space=pltpu.HBM)
    vmem_spec = pl.BlockSpec(memory_space=pltpu.VMEM)
    sem = pltpu.SemaphoreType.DMA
    outs = (
        jax.ShapeDtypeStruct((PART, HEADS * HEAD_DIM), BF16),
        jax.ShapeDtypeStruct((PART, HEADS * HEAD_DIM), BF16),
        jax.ShapeDtypeStruct((PART, KV_HEADS * HEAD_DIM), BF16),
        jax.ShapeDtypeStruct((PART, KV_HEADS * HEAD_DIM), BF16),
    )
    results = pl.pallas_call(
        kernel,
        out_shape=outs,
        in_specs=[hbm_spec] * 5,
        out_specs=(vmem_spec,) * 4,
        scratch_shapes=[
            pltpu.VMEM((PART, HEADS * HEAD_DIM), BF16),
            pltpu.VMEM((PART, HEADS * HEAD_DIM), BF16),
            pltpu.VMEM((PART, KV_HEADS * HEAD_DIM), BF16),
            pltpu.VMEM((PART, KV_HEADS * HEAD_DIM), BF16),
            pltpu.VMEM((TP, PART, WIDE), BF16),
            pltpu.VMEM((TP, PART, WIDE), BF16),
            pltpu.VMEM((BLOCKS, TP, PART, HEAD_DIM), BF16),
            pltpu.VMEM((BLOCKS, TP, PART, HEAD_DIM), BF16),
            pltpu.VMEM((BLOCKS, HEAD_ROWS, 128), BF16),
            pltpu.VMEM((BLOCKS, TOK, HEAD_DIM), BF16),
            pltpu.VMEM((BLOCKS, TOK, HEAD_DIM), BF16),
            pltpu.VMEM((BLOCKS, TOK, PAIR), F32),
            pltpu.VMEM((ALL_ROWS, HEAD_DIM), BF16),
            pltpu.VMEM((ALL_ROWS, HEAD_DIM), BF16),
            pltpu.VMEM((BLOCKS, TOK, ALL_ROWS), F32),
            pltpu.VMEM((BLOCKS, TOK, ALL_ROWS), F32),
            pltpu.VMEM((BLOCKS, 1, ALL_ROWS), F32),
            pltpu.VMEM((BLOCKS, 1, ALL_ROWS), F32),
            pltpu.VMEM((BLOCKS, 1, ALL_ROWS), F32),
            pltpu.VMEM((BLOCKS + 1, 1, ALL_ROWS), F32),
            pltpu.VMEM((BLOCKS, TOK, ALL_ROWS), BF16),
            pltpu.VMEM((BLOCKS, TOK, ALL_ROWS), BF16),
            pltpu.VMEM((2, BLOCKS, TOK, HEAD_DIM), F32),
            pltpu.VMEM((TP, PART, WIDE), BF16),
            pltpu.VMEM((TP, PART, WIDE), BF16),
            pltpu.VMEM((2, TP, PART, HEAD_DIM), BF16),
            pltpu.VMEM((2, TP, PART, HEAD_DIM), BF16),
            pltpu.VMEM((2, TP, PART, HEAD_DIM), BF16),
            pltpu.VMEM((2, TP, PART, HEAD_DIM), BF16),
            pltpu.VMEM((2, SPAN - 1, TOK, HEAD_DIM), BF16),
            pltpu.VMEM((2, SPAN - 1, TOK, HEAD_DIM), BF16),
            pltpu.VMEM((1, TOK), jnp.int32),
            sem((5,)),
            sem((8,)),
            sem((6,)),
            sem((6,)),
            sem((5, SPAN)),
            sem((5, SPAN)),
            sem((4, SPAN - 1)),
            sem((4, SPAN - 1)),
            sem((4,)),
            sem((4,)),
            sem((2,)),
            sem((2,)),
        ],
        compiler_params=pltpu.CompilerParams(
            collective_id=0, has_side_effects=True, vmem_limit_bytes=62 * 1024 * 1024
        ),
    )(query_in, key_in, value_in, grad_out, segments.reshape(1, TOK))
    return pl.pallas_call(
        deliver,
        out_shape=outs,
        in_specs=[vmem_spec] * 4,
        out_specs=(hbm_spec,) * 4,
        scratch_shapes=[sem((4,))],
    )(*results)


def solution(mesh):
    split = P(("ctx", "tp"), None)
    return jax.shard_map(
        body,
        mesh=mesh,
        in_specs=(split, split, split, split, P("ctx")),
        out_specs=(split, split, split, split),
        check_vma=False,
    )
```

time: 68.2 us -> 51.5 us (0.76)
  Pallas kernels: 60.3 us -> 50.7 us
  local copies, waits for them, and re-layouts: 6.99 us -> 0 us
    pallas_call x1 -> x2, Pallas kernels: 60.3 us -> 50.7 us  [the longest x1 48.7 us: body(): pl.pallas_call(kernel, out_shape=outs, in_specs=[hbm_spec] * 5, out_specs...]
    unnamed x14 -> x0, local copies, waits for them, and re-layouts: 6.99 us -> none
where the time goes in v2:
time: 51.5 us; the launch traced here: 51.4 us
  Pallas kernels  50.7 us (98%)
  between operations  0.64 us (1%)
    pallas_call x1, Pallas kernels, body(): pl.pallas_call(kernel, out_shape=outs, in_specs=[hbm_spec] * 5, out_specs...  48.7 us
    pallas_call x1, Pallas kernels, body(): pl.pallas_call(deliver, out_shape=outs, in_specs=[vmem_spec] * 4, out_spe...  2.05 us

profile of v2, /device:TPU:1, one launch (start us, length us, event | category | flops | bytes accessed | tf_op | source)
XLA Modules:
  0.0 51.4 jit_solution(11275528102029700117)
XLA Ops:
  0.6 48.7 %shard_map.84 = (bf16[24,8192]{1,0:T(8,128)(2,1)}, bf16[24,8192]{1,0:T(8,128)(2,1)}, bf16[24,1024]{1,0:T(8,128)(2,1)}, bf16[24,1024]{1,0:T(8,128)(2,1)}) custom-call(bf16[24,8192]{1,0:T(8,128)(2,1)} %q_in.1, bf16[24,1024]{1,0:T(8,128)(2,1)} %k_in.1, bf16[24,1024]{1,0:T(8,128)(2,1)} %v_in.1, bf16[24,8192]{1,0:T(8,128)(2,1)} %g_in.1, s32[1,192]{1,0:T(1,128)} %bitcast.1), custom_call_target="tpu_custom_call" | custom-call | tf_op jit(solution)/shard_map/pallas_call | solution.py:459
  49.3 2.0 %shard_map.85 = (bf16[24,8192]{1,0:T(8,128)(2,1)}, bf16[24,8192]{1,0:T(8,128)(2,1)}, bf16[24,1024]{1,0:T(8,128)(2,1)}, bf16[24,1024]{1,0:T(8,128)(2,1)}) custom-call(bf16[24,8192]{1,0:T(8,128)(2,1)} %get-tuple-element.8.o, bf16[24,8192]{1,0:T(8,128)(2,1)} %get-tuple-element.9.dq, bf16[24,1024]{1,0:T(8,128)(2,1)} %get-tuple-element.10.dk, ...), custom_call_target="tpu_custom_call" | custom-call | tf_op jit(solution)/shard_map/pallas_call | solution.py:514

commit v3 on v2

--- a/solution.py
+++ b/solution.py
@@ -59,7 +59,7 @@
     ob, dqb, near, far, near_in, far_in,
     tx, rx,
     seg_v, load_sem, local_sem, in_send, in_recv, hop_send, hop_recv, back_send, back_recv,
-    out_send, out_recv, end_send, end_recv,
+    out_send, out_recv, end_send, end_recv, present,
 ):
     ctx = lax.axis_index("ctx")
     me = lax.axis_index("tp")
@@ -77,9 +77,13 @@
     barrier = pltpu.get_barrier_semaphore()
 
     def greet(j, carry):
+        peer = lax.rem(me + TP // 2 + j, TP)
+        pl.semaphore_signal(barrier, inc=1, device_id=(before, peer), device_id_type=MESH)
+        return carry
+
+    def greet_on(j, carry):
         peer = lax.rem(me + j, TP)
-        pl.semaphore_signal(barrier, inc=1, device_id=(after, peer), device_id_type=MESH)
-        pl.semaphore_signal(barrier, inc=1, device_id=(before, peer), device_id_type=MESH)
+        pl.semaphore_signal(present, inc=1, device_id=(after, peer), device_id_type=MESH)
         return carry
 
     def greet_near(j, carry):
@@ -89,7 +93,7 @@
 
     lax.fori_loop(0, TP, greet, 0)
     lax.fori_loop(1, TP, greet_near, 0)
-    pl.semaphore_wait(barrier, 3 * TP - 1)
+    pl.semaphore_wait(barrier, 2 * TP - 1)
 
     def columns(owner, width):
         return pl.ds(pl.multiple_of(owner * width, width), width)
@@ -112,7 +116,7 @@
 
     def scatter_on(src, buf, n):
         def send(j, carry):
-            peer = lax.rem(me + j, TP)
+            peer = lax.rem(me + TP // 2 + j, TP)
             pltpu.make_async_remote_copy(
                 src_ref=src.at[:, columns(peer, HEAD_DIM)],
                 dst_ref=buf.at[1, me],
@@ -160,7 +164,6 @@
                 pass_on(buf.at[d, part], buf.at[d + 1, part], 2 * n + c, d)
 
     def hop_keys(d):
-        hop_ids(d)
         hop(kc, d, 0)
 
     def hop_values(d):
@@ -188,7 +191,6 @@
         return kx[d]
 
     def score(d):
-        make_bias(d)
         kx[d] = joined(kc.at[d], 0)
         s = dot(keys(d), qp[...], NT)
         for lanes, cover in zip(tiles, bias_tiles):
@@ -199,8 +201,10 @@
             tops[d, :, lanes] = top
             sums[d, :, lanes] = jnp.sum(e, axis=0, keepdims=True)
 
+    def take_values(d):
+        vx[d] = joined(vc.at[d], 0)
+
     def dprob(d):
-        vx[d] = joined(vc.at[d], 0)
         t = dot(vx[d], gp[...], NT)
         for lanes in tiles:
             dp = t[:, lanes]
@@ -296,39 +300,36 @@
             total = near_in[n, h].astype(F32) + far_in[n, h].astype(F32)
             dst[:, h * HEAD_DIM : (h + 1) * HEAD_DIM] = total.astype(BF16)
 
-    def give(buf, dst, width, n):
-        def send(j, carry):
-            peer = lax.rem(me + j, TP)
-            pltpu.make_async_remote_copy(
-                src_ref=buf.at[peer],
-                dst_ref=dst.at[:, columns(me, width)],
-                send_sem=out_send.at[n],
-                recv_sem=out_recv.at[n],
-                device_id=(ctx, peer),
-                device_id_type=MESH,
-            ).start()
-            return carry
-
-        lax.fori_loop(1, TP, send, 0)
-        pltpu.make_async_copy(
-            buf.at[me], dst.at[:, columns(me, width)], local_sem.at[4 + n]
-        ).start()
-
-    def product(parts, low, scaling, buf, dst, n):
-        for h in range(0, GROUPS, 2):
-            lanes = slice(h * TOK, h * TOK + PAIR)
-            total = None
-            for d in range(BLOCKS):
-                one = dot(low(d), parts[d, :, lanes])
-                total = one if total is None else total + one
-            both = (total * scaling).T
-            for i in range(2):
-                for r in range(TP):
-                    start = i * TOK + r * PART
-                    buf[r, :, (h + i) * HEAD_DIM : (h + i + 1) * HEAD_DIM] = both[
-                        start : start + PART
-                    ].astype(BF16)
-        give(buf, dst, WIDE, n)
+    def product(parts, low, scaling, buf, dst, n, cuts):
+        turned = [low(d).astype(F32).T.astype(BF16) for d in range(BLOCKS)]
+        for cut in range(cuts):
+            for h in range(cut * GROUPS // cuts, (cut + 1) * GROUPS // cuts, 2):
+                lanes = slice(h * TOK, h * TOK + PAIR)
+                total = sum(dot(turned[d], parts[d, :, lanes]) for d in range(BLOCKS))
+                both = (total * scaling).T
+                for i in range(2):
+                    for r in range(TP):
+                        start = i * TOK + r * PART
+                        buf[r, :, (h + i) * HEAD_DIM : (h + i + 1) * HEAD_DIM] = both[
+                            start : start + PART
+                        ].astype(BF16)
+            size = WIDE // cuts
+
+            def send(j, carry, cut=cut, size=size):
+                peer = lax.rem(me + j, TP)
+                lanes = pl.ds(pl.multiple_of(me * WIDE + cut * size, HEAD_DIM), size)
+                pltpu.make_async_remote_copy(
+                    src_ref=buf.at[peer, :, pl.ds(cut * size, size)],
+                    dst_ref=dst.at[:, lanes],
+                    send_sem=out_send.at[n],
+                    recv_sem=out_recv.at[n],
+                    device_id=(ctx, peer),
+                    device_id_type=MESH,
+                ).start()
+                return carry
+
+            lax.fori_loop(1, TP, send, 0)
+        pltpu.make_async_copy(buf.at[me], dst.at[:, columns(me, WIDE)], local_sem.at[4 + n]).start()
 
     def drain():
         for n, (buf, dst) in enumerate(((ob, o_out), (dqb, dq_out))):
@@ -360,18 +361,23 @@
     head = jnp.where(place == 0, ids[:, :128], jnp.where(place == 1, late_ids, 0.0))
     sg[0] = head.astype(BF16)
     loads[0].wait()
-    loads[1].wait()
     scatter_on(ks, kc, 4)
     hop_ids(0)
     scatter(ks, kc.at[0], HEAD_DIM, 0)
+    loads[1].wait()
     scatter_on(vs, vc, 5)
     scatter(vs, vc.at[0], HEAD_DIM, 1)
     loads[2].wait()
     scatter(qs, qb, WIDE, 2)
+    lax.fori_loop(0, TP, greet_on, 0)
+    hop_ids(1)
     hop_keys(1)
     hop_values(1)
     loads[3].wait()
     scatter(gs, gb, WIDE, 3)
+    make_bias(0)
+    make_bias(1)
+    hop_ids(2)
     hop_keys(2)
     hop_values(2)
     gathered(qb, 2)
@@ -379,45 +385,52 @@
         qp[h * TOK : (h + 1) * TOK, :] = joined(qb, h * HEAD_DIM)
     gathered(kc.at[0], 0)
     score(0)
+    hop_ids(3)
     hop_keys(3)
     score(1)
     hop_values(3)
+    make_bias(2)
     score(2)
+    make_bias(3)
     score(3)
+    hop_ids(4)
+    make_bias(4)
     gathered(gb, 3)
     for h in range(GROUPS):
         gp[h * TOK : (h + 1) * TOK, :] = joined(gb, h * HEAD_DIM)
     gathered(vc.at[0], 1)
+    take_values(0)
     dprob(0)
+    take_values(1)
     dprob(1)
+    take_values(2)
     dprob(2)
+    take_values(3)
     dprob(3)
     hop_keys(4)
     score(4)
     combine()
     weigh(4)
     value_term(4)
+    pl.semaphore_wait(present, TP)
     back(0, 0)
-    weigh(3)
-    weigh(2)
+    for d in range(SPAN):
+        weigh(d)
     hop_values(4)
+    take_values(4)
     dprob(4)
     combine_dots()
+    product(pb, lambda d: vx[d], 1.0, ob, o_out, 0, 2)
     weigh_keys(4)
     key_term(4)
     back(0, 1)
-    weigh(1)
-    weigh(0)
-    product(pb, lambda d: vx[d].astype(F32).T.astype(BF16), 1.0, ob, o_out, 0)
+    for d in range(SPAN):
+        weigh_keys(d)
+    product(db, lambda d: keys(d), SCALE, dqb, dq_out, 1, 2)
     value_term(3)
     back(1, 0)
-    weigh_keys(3)
     key_term(3)
     back(1, 1)
-    weigh_keys(2)
-    weigh_keys(1)
-    weigh_keys(0)
-    product(db, lambda d: keys(d).astype(F32).T.astype(BF16), SCALE, dqb, dq_out, 1)
     value_term(2)
     back(2, 0)
     key_term(2)
@@ -435,15 +448,17 @@
     drain()
 
 
-def deliver(o, dq, dk, dv, o_out, dq_out, dk_out, dv_out, sems):
-    copies = [
-        pltpu.make_async_copy(src, dst, sems.at[n])
-        for n, (src, dst) in enumerate(((o, o_out), (dq, dq_out), (dk, dk_out), (dv, dv_out)))
-    ]
-    for copy in copies:
-        copy.start()
-    for copy in copies:
-        copy.wait()
+def deliver(o, dq, dk, dv, o_out, dq_out, dk_out, dv_out, ov, dqv, dkv, dvv, in_sems, out_sems):
+    rows = ((o, ov, o_out), (dq, dqv, dq_out), (dk, dkv, dk_out), (dv, dvv, dv_out))
+    fetches = [pltpu.make_async_copy(a, b, in_sems.at[n]) for n, (a, b, _) in enumerate(rows)]
+    writes = [pltpu.make_async_copy(b, c, out_sems.at[n]) for n, (_, b, c) in enumerate(rows)]
+    for fetch in fetches:
+        fetch.start()
+    for fetch, write in zip(fetches, writes):
+        fetch.wait()
+        write.start()
+    for write in writes:
+        write.wait()
 
 
 def body(query_in, key_in, value_in, grad_out, segments):
@@ -506,6 +521,7 @@
             sem((4,)),
             sem((2,)),
             sem((2,)),
+            pltpu.SemaphoreType.REGULAR,
         ],
         compiler_params=pltpu.CompilerParams(
             collective_id=0, has_side_effects=True, vmem_limit_bytes=62 * 1024 * 1024
@@ -514,9 +530,10 @@
     return pl.pallas_call(
         deliver,
         out_shape=outs,
-        in_specs=[vmem_spec] * 4,
+        in_specs=[hbm_spec] * 4,
         out_specs=(hbm_spec,) * 4,
-        scratch_shapes=[sem((4,))],
+        scratch_shapes=[pltpu.VMEM(out.shape, BF16) for out in outs] + [sem((4,)), sem((4,))],
+        compiler_params=pltpu.CompilerParams(vmem_limit_bytes=62 * 1024 * 1024),
     )(*results)
 
 

time: 51.5 us -> 49.7 us (0.965)
  Pallas kernels: 50.7 us -> 48.9 us
    pallas_call x1, Pallas kernels: 48.7 us -> 46.9 us  [body(): pl.pallas_call(kernel, out_shape=outs, in_specs=[hbm_spec] * 5, out_specs...]
where the time goes in v3:
time: 49.7 us; the launch traced here: 49.5 us
  Pallas kernels  48.9 us (98%)
  between operations  0.64 us (1%)
    pallas_call x1, Pallas kernels, body(): pl.pallas_call(kernel, out_shape=outs, in_specs=[hbm_spec] * 5, out_specs...  46.9 us
    pallas_call x1, Pallas kernels, body(): pl.pallas_call(deliver, out_shape=outs, in_specs=[hbm_spec] * 4, out_spec...  1.96 us

profile of v3, /device:TPU:1, one launch (start us, length us, event | category | flops | bytes accessed | tf_op | source)
XLA Modules:
  0.0 49.5 jit_solution(12775989840337586500)
XLA Ops:
  0.6 46.9 %shard_map.84 = (bf16[24,8192]{1,0:T(8,128)(2,1)}, bf16[24,8192]{1,0:T(8,128)(2,1)}, bf16[24,1024]{1,0:T(8,128)(2,1)}, bf16[24,1024]{1,0:T(8,128)(2,1)}) custom-call(bf16[24,8192]{1,0:T(8,128)(2,1)} %q_in.1, bf16[24,1024]{1,0:T(8,128)(2,1)} %k_in.1, bf16[24,1024]{1,0:T(8,128)(2,1)} %v_in.1, bf16[24,8192]{1,0:T(8,128)(2,1)} %g_in.1, s32[1,192]{1,0:T(1,128)} %bitcast.1), custom_call_target="tpu_custom_call" | custom-call | tf_op jit(solution)/shard_map/pallas_call | solution.py:474
  47.5 2.0 %shard_map.85 = (bf16[24,8192]{1,0:T(8,128)(2,1)}, bf16[24,8192]{1,0:T(8,128)(2,1)}, bf16[24,1024]{1,0:T(8,128)(2,1)}, bf16[24,1024]{1,0:T(8,128)(2,1)}) custom-call(bf16[24,8192]{1,0:T(8,128)(2,1)} %get-tuple-element.8.o, bf16[24,8192]{1,0:T(8,128)(2,1)} %get-tuple-element.9.dq, bf16[24,1024]{1,0:T(8,128)(2,1)} %get-tuple-element.10.dk, ...), custom_call_target="tpu_custom_call" | custom-call | tf_op jit(solution)/shard_map/pallas_call | solution.py:530
